TPU v7x, 32 devices: a whole 2x2x4 slice. The times are simulated.
32 devices in a mesh: groups: 2 (over x), band: 16 (over z, y, core).
Axes of the slice: x: 2, y: 2, z: 4, core: 2. Of those that a mesh axis runs over, the one named last changes fastest.
Arguments:
- grid_rows: bfloat16 [16384, 1024], P(('groups', 'band')), parts along dimension 0, may hold values from -6 to 6
- row_slot: int32 [16384], P(('groups', 'band')), parts along dimension 0, may hold values from -1 to 511, as said below
- band_counts: int32 [32, 16], P('groups'), parts along dimension 0, may hold values from 1 to 32, as said below
- norm_gain: float32 [1024], replicated, may hold values from 0.1 to 1.9
- w_qkv: bfloat16 [1024, 3072], replicated
- w_out: bfloat16 [1024, 1024], replicated, may hold values from -0.1875 to 0.1875
Outputs:
- update: bfloat16 [16384, 1024], P(('groups', 'band')), parts along dimension 0
There are 2 independent parts, one for each index of `groups`. A program takes and returns all parts, laid end to end along the dimension named above; an argument that names none is the same for every part. Nothing has to cross between parts.
Inputs may be any that keep to these rules, and one draw needn't show every extreme that they name: `row_slot`: values b * 32 + c of one owner's rows are distinct; the owner s holds exactly band_counts[s, b] rows with slots b * 32 + c, namely those with c < band_counts[s, b]; the other rows hold -1. `band_counts`: some band receives 32 rows from every owner.
All inputs are finite; a program needn't handle non-finite values.
Results may differ from a plain program's by a relative error of at most 0.009.
Values may be sent and summed in bfloat16 or wider, within the bound.
A program may use at most 64 MiB of HBM per device.

v0:
```python
import jax
import jax.numpy as jnp
from jax import lax
from jax.sharding import PartitionSpec as P

HEADS = 16


def with_halo(array, sides, width):
    for axis, dim in sides:
        peers, length = (lax.axis_size(axis), array.shape[dim])
        up = [(i, (i + 1) % peers) for i in range(peers - 1)]
        down = [(j, i) for i, j in up]
        last = lax.slice_in_dim(array, length - width, length, axis=dim)
        initial = lax.slice_in_dim(array, 0, width, axis=dim)
        before = lax.ppermute(last, axis, up)
        after = lax.ppermute(initial, axis, down)
        array = jnp.concatenate([before, array, after], axis=dim)
    return array


def normalize(rows_in, norm_gain):
    values = rows_in.astype(jnp.float32)
    center = jnp.mean(values, axis=-1, keepdims=True)
    spread = jnp.mean((values - center) ** 2, axis=-1, keepdims=True)
    return ((values - center) * lax.rsqrt(spread + 1e-05) * norm_gain).astype(jnp.bfloat16)


def attend(query, wide, key_alive, query_alive, w_out):
    row_count, feat_width = query.shape
    window = (wide.shape[0] - row_count) // 2
    head_dim = feat_width // HEADS
    group_count = HEADS // 4
    distance = (
        jnp.arange(wide.shape[0], dtype=jnp.int32)[None, :]
        - window
        - jnp.arange(row_count, dtype=jnp.int32)[:, None]
    )
    allowed = (jnp.abs(distance) <= window) & key_alive[None, :]
    queries = query.reshape(row_count, group_count, 4, head_dim).transpose(1, 0, 2, 3)
    keys = wide[:, :feat_width].reshape(-1, group_count, 4, head_dim).transpose(1, 0, 2, 3)
    values = wide[:, feat_width:].reshape(-1, group_count, 4, head_dim).transpose(1, 0, 2, 3)

    def one_group(operands):
        query_group, key_group, value_group = operands
        scores = jnp.einsum(
            "qhd,khd->hqk", query_group, key_group, preferred_element_type=jnp.float32
        ) * head_dim ** (-0.5)
        scores = jnp.where(allowed[None], scores, -1e30)
        highest = jnp.max(scores, axis=-1, keepdims=True)
        exponent = jnp.exp(scores - highest)
        weights = (exponent / jnp.sum(exponent, axis=-1, keepdims=True)).astype(jnp.bfloat16)
        blended = jnp.einsum(
            "hqk,khd->qhd", weights, value_group, preferred_element_type=jnp.float32
        )
        return blended.astype(jnp.bfloat16)

    mixed = lax.map(one_group, (queries, keys, values))
    mixed = mixed.transpose(1, 0, 2, 3).reshape(row_count, feat_width)
    update = jnp.dot(mixed, w_out, preferred_element_type=jnp.float32)
    return jnp.where(query_alive[:, None], update, 0.0).astype(jnp.bfloat16)


def body(grid_rows, row_slot, band_counts, norm_gain, w_qkv, w_out):
    row_count, feat_width = grid_rows.shape
    band_total = lax.axis_size("band")
    slot_cap = row_count // band_total
    window = row_count // 4
    slot_iota = jnp.arange(row_count, dtype=jnp.int32)
    onehot_table = (row_slot[:, None] == slot_iota[None, :]).astype(jnp.bfloat16)
    outgoing = lax.dot_general(
        onehot_table, grid_rows, (((0,), (0,)), ((), ())), preferred_element_type=jnp.float32
    ).astype(jnp.bfloat16)
    outgoing = outgoing.reshape(band_total, slot_cap, feat_width)
    normed_part = normalize(
        lax.all_to_all(outgoing, "band", split_axis=0, concat_axis=0, tiled=True), norm_gain
    )
    qkv_part = jnp.einsum(
        "scd,de->sce", normed_part, w_qkv, preferred_element_type=jnp.float32
    ).astype(jnp.bfloat16)
    normed = normed_part
    qkv = qkv_part
    normed = normed.reshape(row_count, feat_width)
    qkv = qkv.reshape(row_count, 3 * feat_width)
    query = qkv[:, :feat_width]
    keyval = qkv[:, feat_width:]
    wide = with_halo(keyval, (("band", 0),), window)
    band_here = lax.axis_index("band")
    cap_iota = jnp.arange(slot_cap, dtype=jnp.int32)

    def alive_of(which_band):
        inside = (which_band >= 0) & (which_band < band_total)
        clamped = jnp.clip(which_band, 0, band_total - 1)
        column = lax.dynamic_slice_in_dim(band_counts, clamped, 1, 1)[:, 0]
        return ((cap_iota[None, :] < column[:, None]) & inside).reshape(-1)

    query_alive = alive_of(band_here)
    key_alive = jnp.concatenate(
        [alive_of(band_here - 1)[-window:], query_alive, alive_of(band_here + 1)[:window]], 0
    )
    return attend(query, wide, key_alive, query_alive, w_out)


def solution(mesh):
    return jax.shard_map(
        body,
        mesh=mesh,
        in_specs=(
            P(("groups", "band"), None),
            P(("groups", "band")),
            P("groups", None),
            P(),
            P(),
            P(),
        ),
        out_specs=P(("groups", "band"), None),
        check_vma=False,
    )
```

profile of v0, /device:TPU:19, one launch (start us, length us, event | category | flops | bytes accessed | tf_op | source)
XLA Modules:
  0.0 120.6 jit_solution(5955096728472651007)
XLA Ops:
  0.0 3.2 %convolution_convert_fusion = bf16[512,1024]{1,0:T(8,128)(2,1)} fusion(bf16[512,1024]{1,0:T(8,128)(2,1)} %param.8, s32[512]{0:T(512)} %param.9), kind=kOutput, calls=%fused_computation.44 | convolution fusion | flops 537657344 | bytes 2099200 | tf_op jit(solution)/shard_map/dot_general | solution.py:71
  3.2 6.6 %all-to-all-start = ((bf16[16,32,1024]{2,1,0:T(8,128)(2,1)}), bf16[16,32,1024]{2,1,0:T(8,128)(2,1)S(1)}, u32[]{:S(2)}, u32[]{:S(2)}) async-start(bf16[16,32,1024]{2,1,0:T(8,128)(2,1)} %bitcast.70), calls=%async_computation | async-start | bytes 2097152 | tf_op jit(solution)/shard_map/all_to_all | solution.py:76
  10.2 24.3 %all-to-all-done = bf16[16,32,1024]{2,1,0:T(8,128)(2,1)S(1)} async-done(((bf16[16,32,1024]{2,1,0:T(8,128)(2,1)}), bf16[16,32,1024]{2,1,0:T(8,128)(2,1)S(1)}, u32[]{:S(2)}, u32[]{:S(2)}) %all-to-all-start) | async-done | bytes 1048608 | tf_op jit(solution)/shard_map/all_to_all | solution.py:76
  34.7 0.4 fusion.49
  35.2 6.6 %fusion.44 = bf16[16,32,3072]{2,1,0:T(8,128)(2,1)S(1)} fusion(bf16[1024,3072]{1,0:T(8,128)(2,1)} %param.12, bf16[16,32,1024]{2,1,0:T(8,128)(2,1)S(1)} %all-to-all-done, f32[1024]{0:T(1024)S(1)} %copy-done.3, f32[16,32]{1,0:T(8,128)S(1)} %add_rsqrt_fusion, f32[16,32]{1,0:T(8,128)S(1)} %broadcast_multiply_fusion), kind=kOutput, calls=%fused_computation.34 | convolution fusion | flops 3225419776 | bytes 10493952 | tf_op jit(solution)/shard_map/scd,de->sce/dot_general | solution.py:78
  41.8 1.7 %copy-done.1 = bf16[16,32,3072]{2,1,0:T(8,128)(2,1)} copy-done((bf16[16,32,3072]{2,1,0:T(8,128)(2,1)}, bf16[16,32,3072]{2,1,0:T(8,128)(2,1)S(1)}, u32[]{:S(2)}) %copy-start.1) | copy-done | bytes 3145752
  43.5 1.1 fusion.70
  44.6 2.1 %collective-permute-start = (bf16[128,2048]{1,0:T(8,128)(2,1)}, bf16[128,2048]{1,0:T(8,128)(2,1)}, u32[]{:S(2)}, u32[]{:S(2)}) collective-permute-start(bf16[128,2048]{1,0:T(8,128)(2,1)} %get-tuple-element.77), channel_id=1, source_target_pairs={{0,1},{1,2},{2,3},{3,4},{4,5},{5,6},{6,7},{7,8},{8,9},{9,10},{10,1... | collective-permute-start | bytes 1572872 | tf_op jit(solution)/shard_map/ppermute | solution.py:16
  46.6 2.6 %collective-permute-start.1 = (bf16[128,2048]{1,0:T(8,128)(2,1)}, bf16[128,2048]{1,0:T(8,128)(2,1)}, u32[]{:S(2)}, u32[]{:S(2)}) collective-permute-start(bf16[128,2048]{1,0:T(8,128)(2,1)} %get-tuple-element.78), channel_id=1, source_target_pairs={{1,0},{2,1},{3,2},{4,3},{5,4},{6,5},{7,6},{8,7},{9,8},{10,9},{11,1... | collective-permute-start | bytes 1572872 | tf_op jit(solution)/shard_map/ppermute | solution.py:17
  49.7 3.2 %slice.43 = bf16[512,2048]{1,0:T(8,128)(2,1)} slice(bf16[512,3072]{1,0:T(8,128)(2,1)} %bitcast.65), slice={[0:512], [1024:3072]} | slice | bytes 4194304 | tf_op jit(solution)/shard_map/slice | solution.py:86
  52.9 1.3 %slice.46 = bf16[512,1024]{1,0:T(8,128)(2,1)S(1)} slice(bf16[512,3072]{1,0:T(8,128)(2,1)} %bitcast.66), slice={[0:512], [0:1024]} | slice | bytes 2097152 | tf_op jit(solution)/shard_map/slice | solution.py:85
  54.2 1.3 %copy.11 = bf16[512,1024]{0,1:T(8,128)(2,1)} copy(bf16[512,1024]{1,0:T(8,128)(2,1)S(1)} %slice.46) | data formatting | bytes 2097152 | tf_op jit(solution)/shard_map/slice | solution.py:85
  55.6 3.1 %collective-permute-done = bf16[128,2048]{1,0:T(8,128)(2,1)} collective-permute-done((bf16[128,2048]{1,0:T(8,128)(2,1)}, bf16[128,2048]{1,0:T(8,128)(2,1)}, u32[]{:S(2)}, u32[]{:S(2)}) %collective-permute-start) | collective-permute-done | bytes 524320 | tf_op jit(solution)/shard_map/ppermute | solution.py:16
  58.7 3.4 %collective-permute-done.1 = bf16[128,2048]{1,0:T(8,128)(2,1)} collective-permute-done((bf16[128,2048]{1,0:T(8,128)(2,1)}, bf16[128,2048]{1,0:T(8,128)(2,1)}, u32[]{:S(2)}, u32[]{:S(2)}) %collective-permute-start.1) | collective-permute-done | bytes 524320 | tf_op jit(solution)/shard_map/ppermute | solution.py:17
  62.1 2.0 %pad_maximum_fusion = bf16[768,2048]{1,0:T(8,128)(2,1)S(1)} fusion(bf16[128,2048]{1,0:T(8,128)(2,1)} %collective-permute-done.1, bf16[512,2048]{1,0:T(8,128)(2,1)} %slice.43, bf16[128,2048]{1,0:T(8,128)(2,1)} %collective-permute-done), kind=kLoop, calls=%fused_computation.35 | loop fusion | flops 9437184 | bytes 6291456 | tf_op jit(solution)/shard_map/concatenate | solution.py:18
  64.1 2.0 %fusion.69 = (bf16[768,1024]{1,0:T(8,128)(2,1)}, bf16[768,1024]{1,0:T(8,128)(2,1)}) fusion(bf16[768,2048]{1,0:T(8,128)(2,1)S(1)} %pad_maximum_fusion), kind=kLoop, calls=%fused_computation.64 | loop fusion | bytes 6291456 | tf_op jit(solution)/shard_map/slice | solution.py:41
  66.1 2.6 %copy.10 = bf16[768,1024]{0,1:T(8,128)(2,1)} copy(bf16[768,1024]{1,0:T(8,128)(2,1)} %get-tuple-element.76) | data formatting | bytes 3145728 | tf_op jit(solution)/shard_map/slice | solution.py:42
  68.7 2.7 %copy.12 = bf16[768,1024]{0,1:T(8,128)(2,1)} copy(bf16[768,1024]{1,0:T(8,128)(2,1)} %get-tuple-element.75) | data formatting | bytes 3145728 | tf_op jit(solution)/shard_map/slice | solution.py:41
  71.3 45.8 %while.11 = (s32[]{:T(128)}, bf16[4,512,4,64]{1,3,2,0:T(8,128)(2,1)}, bf16[4,768,4,64]{1,3,2,0:T(8,128)(2,1)}, bf16[4,512,4,64]{1,3,2,0:T(8,128)(2,1)}, bf16[4,7...) while((s32[]{:T(128)}, ...), condition=%wide.region_5.6_spmd.clone, body=%wide.region_2.5_spmd.clone.sunk | while | flops 413795072 | bytes 14702421 | solution.py:58
  71.3 0.5 fusion.83
  71.8 6.2 %fusion.84 = (f32[4,512]{1,0:T(4,128)S(1)}, f32[4,512,768]{2,1,0:T(8,128)}) fusion(pred[512,768]{1,0:T(8,128)(4,1)S(1)} %fusion.83, bf16[4,768,4,64]{1,3,2,0:T(8,128)(2,1)} %get-tuple-element.146, s32[]{:T(128)} %get-tuple-element.134, bf16[4,512,4,64]{1,3,2,0:T(8,128)(2,1)} %get-tuple-element.145), kind=kOutput, calls=%fused_computation.63.clone.1 | convolution fusion | flops 207618816 | bytes 7349248 | tf_op jit(solution)/shard_map/while/body/eval_jaxpr/sub | solution.py:51
  78.0 4.8 %fusion.85 = bf16[4,512,4,64]{1,3,2,0:T(8,128)(2,1)} fusion(bf16[4,512,4,64]{1,3,2,0:T(8,128)(2,1)} %get-tuple-element.135, s32[]{:T(128)} %get-tuple-element.134, f32[4,512,768]{2,1,0:T(8,128)} %get-tuple-element.124, f32[4,512]{1,0:T(4,128)S(1)} %get-tuple-element.125, bf16[4,768,4,64]{1,3,2,0:T(8,128)(2,1)} %get-tuple-element.144), kind=kOutput, calls=%fused_computation.14.clone.1 | convolution fusion | flops 204603392 | bytes 6956032 | tf_op jit(solution)/shard_map/while/body/eval_jaxpr/hqk,khd->qhd/dot_general | solution.py:53
  82.8 0.5 fusion.83
  83.2 6.2 %fusion.84 = (f32[4,512]{1,0:T(4,128)S(1)}, f32[4,512,768]{2,1,0:T(8,128)}) fusion(pred[512,768]{1,0:T(8,128)(4,1)S(1)} %fusion.83, bf16[4,768,4,64]{1,3,2,0:T(8,128)(2,1)} %get-tuple-element.146, s32[]{:T(128)} %get-tuple-element.134, bf16[4,512,4,64]{1,3,2,0:T(8,128)(2,1)} %get-tuple-element.145), kind=kOutput, calls=%fused_computation.63.clone.1 | convolution fusion | flops 207618816 | bytes 7349248 | tf_op jit(solution)/shard_map/while/body/eval_jaxpr/sub | solution.py:51
  89.4 4.8 %fusion.85 = bf16[4,512,4,64]{1,3,2,0:T(8,128)(2,1)} fusion(bf16[4,512,4,64]{1,3,2,0:T(8,128)(2,1)} %get-tuple-element.135, s32[]{:T(128)} %get-tuple-element.134, f32[4,512,768]{2,1,0:T(8,128)} %get-tuple-element.124, f32[4,512]{1,0:T(4,128)S(1)} %get-tuple-element.125, bf16[4,768,4,64]{1,3,2,0:T(8,128)(2,1)} %get-tuple-element.144), kind=kOutput, calls=%fused_computation.14.clone.1 | convolution fusion | flops 204603392 | bytes 6956032 | tf_op jit(solution)/shard_map/while/body/eval_jaxpr/hqk,khd->qhd/dot_general | solution.py:53
  94.2 0.5 fusion.83
  94.7 6.2 %fusion.84 = (f32[4,512]{1,0:T(4,128)S(1)}, f32[4,512,768]{2,1,0:T(8,128)}) fusion(pred[512,768]{1,0:T(8,128)(4,1)S(1)} %fusion.83, bf16[4,768,4,64]{1,3,2,0:T(8,128)(2,1)} %get-tuple-element.146, s32[]{:T(128)} %get-tuple-element.134, bf16[4,512,4,64]{1,3,2,0:T(8,128)(2,1)} %get-tuple-element.145), kind=kOutput, calls=%fused_computation.63.clone.1 | convolution fusion | flops 207618816 | bytes 7349248 | tf_op jit(solution)/shard_map/while/body/eval_jaxpr/sub | solution.py:51
  100.9 4.8 %fusion.85 = bf16[4,512,4,64]{1,3,2,0:T(8,128)(2,1)} fusion(bf16[4,512,4,64]{1,3,2,0:T(8,128)(2,1)} %get-tuple-element.135, s32[]{:T(128)} %get-tuple-element.134, f32[4,512,768]{2,1,0:T(8,128)} %get-tuple-element.124, f32[4,512]{1,0:T(4,128)S(1)} %get-tuple-element.125, bf16[4,768,4,64]{1,3,2,0:T(8,128)(2,1)} %get-tuple-element.144), kind=kOutput, calls=%fused_computation.14.clone.1 | convolution fusion | flops 204603392 | bytes 6956032 | tf_op jit(solution)/shard_map/while/body/eval_jaxpr/hqk,khd->qhd/dot_general | solution.py:53
  105.7 0.5 fusion.83
  106.2 6.2 %fusion.84 = (f32[4,512]{1,0:T(4,128)S(1)}, f32[4,512,768]{2,1,0:T(8,128)}) fusion(pred[512,768]{1,0:T(8,128)(4,1)S(1)} %fusion.83, bf16[4,768,4,64]{1,3,2,0:T(8,128)(2,1)} %get-tuple-element.146, s32[]{:T(128)} %get-tuple-element.134, bf16[4,512,4,64]{1,3,2,0:T(8,128)(2,1)} %get-tuple-element.145), kind=kOutput, calls=%fused_computation.63.clone.1 | convolution fusion | flops 207618816 | bytes 7349248 | tf_op jit(solution)/shard_map/while/body/eval_jaxpr/sub | solution.py:51
  112.3 4.8 %fusion.85 = bf16[4,512,4,64]{1,3,2,0:T(8,128)(2,1)} fusion(bf16[4,512,4,64]{1,3,2,0:T(8,128)(2,1)} %get-tuple-element.135, s32[]{:T(128)} %get-tuple-element.134, f32[4,512,768]{2,1,0:T(8,128)} %get-tuple-element.124, f32[4,512]{1,0:T(4,128)S(1)} %get-tuple-element.125, bf16[4,768,4,64]{1,3,2,0:T(8,128)(2,1)} %get-tuple-element.144), kind=kOutput, calls=%fused_computation.14.clone.1 | convolution fusion | flops 204603392 | bytes 6956032 | tf_op jit(solution)/shard_map/while/body/eval_jaxpr/hqk,khd->qhd/dot_general | solution.py:53
  117.1 3.5 %select_convert_fusion = bf16[512,1024]{1,0:T(8,128)(2,1)} fusion(bf16[512,1024]{0,1:T(8,128)(2,1)} %bitcast.72, bf16[1024,1024]{1,0:T(8,128)(2,1)S(1)} %copy-done, pred[512]{0:T(512)(128)(4,1)S(1)} %and.47), kind=kOutput, calls=%fused_computation.43 | convolution fusion | flops 1074790400 | bytes 4194816 | tf_op jit(solution)/shard_map/dot_general | solution.py:60
  (21 shorter events, 1.0 us)
Async XLA Ops:
  0.0 117.1 %copy-start = (bf16[1024,1024]{1,0:T(8,128)(2,1)S(1)}, bf16[1024,1024]{1,0:T(8,128)(2,1)}, u32[]{:S(2)}) copy-start(bf16[1024,1024]{1,0:T(8,128)(2,1)} %param.13) | copy-start | bytes 6291460
  0.0 9.8 %copy-start.2 = (s32[16,16]{1,0:T(8,128)S(1)}, s32[16,16]{1,0:T(8,128)}, u32[]{:S(2)}) copy-start(s32[16,16]{1,0:T(8,128)} %param.10) | copy-start | bytes 3076
  3.2 32.0 %copy-start.3 = (f32[1024]{0:T(1024)S(1)}, f32[1024]{0:T(1024)}, u32[]{:S(2)}) copy-start(f32[1024]{0:T(1024)} %param.11) | copy-start | bytes 12292
  3.2 31.3 %all-to-all-start = ((bf16[16,32,1024]{2,1,0:T(8,128)(2,1)}), bf16[16,32,1024]{2,1,0:T(8,128)(2,1)S(1)}, u32[]{:S(2)}, u32[]{:S(2)}) async-start(bf16[16,32,1024]{2,1,0:T(8,128)(2,1)} %bitcast.70), calls=%async_computation | async-start | bytes 2097152 | tf_op jit(solution)/shard_map/all_to_all | solution.py:76
  41.8 1.7 %copy-start.1 = (bf16[16,32,3072]{2,1,0:T(8,128)(2,1)}, bf16[16,32,3072]{2,1,0:T(8,128)(2,1)S(1)}, u32[]{:S(2)}) copy-start(bf16[16,32,3072]{2,1,0:T(8,128)(2,1)S(1)} %fusion.44) | copy-start | bytes 9437188
  44.6 14.1 %collective-permute-start = (bf16[128,2048]{1,0:T(8,128)(2,1)}, bf16[128,2048]{1,0:T(8,128)(2,1)}, u32[]{:S(2)}, u32[]{:S(2)}) collective-permute-start(bf16[128,2048]{1,0:T(8,128)(2,1)} %get-tuple-element.77), channel_id=1, source_target_pairs={{0,1},{1,2},{2,3},{3,4},{4,5},{5,6},{6,7},{7,8},{8,9},{9,10},{10,1... | collective-permute-start | bytes 1572872 | tf_op jit(solution)/shard_map/ppermute | solution.py:16
  46.6 15.4 %collective-permute-start.1 = (bf16[128,2048]{1,0:T(8,128)(2,1)}, bf16[128,2048]{1,0:T(8,128)(2,1)}, u32[]{:S(2)}, u32[]{:S(2)}) collective-permute-start(bf16[128,2048]{1,0:T(8,128)(2,1)} %get-tuple-element.78), channel_id=1, source_target_pairs={{1,0},{2,1},{3,2},{4,3},{5,4},{6,5},{7,6},{8,7},{9,8},{10,9},{11,1... | collective-permute-start | bytes 1572872 | tf_op jit(solution)/shard_map/ppermute | solution.py:17
where the time goes:
time: 121 us
  matrix products  57.1 us (47%)
  waiting for transfers between devices  30.8 us (25%)
  local copies, waits for them, and re-layouts  16.4 us (14%)
  starting transfers between devices  11.3 us (9%)
  other arithmetic  4.82 us (4%)
    sub x4, matrix products, one_group(): exponent = jnp.exp(scores - highest)  24.6 us
    all_to_all x1, waiting for transfers between devices, body(): lax.all_to_all(outgoing, 'band', split_axis=0, concat_axis=0, tiled=True)  24.3 us
    dot_general x4, matrix products, one_group(): jnp.einsum('hqk,khd->qhd', weights, value_group, preferred_element_type=j...  19.2 us
    all_to_all x1, starting transfers between devices, body(): lax.all_to_all(outgoing, 'band', split_axis=0, concat_axis=0, tiled=True)  6.63 us
    dot_general x1, matrix products, body(): jnp.einsum('scd,de->sce', normed_part, w_qkv, preferred_element_type=jnp....  6.63 us
    slice x2, local copies, waits for them, and re-layouts, attend(): wide[:, :feat_width].reshape(-1, group_count, 4, head_dim)  4.66 us
    dot_general x1, matrix products, attend(): update = jnp.dot(mixed, w_out, preferred_element_type=jnp.float32)  3.46 us
    ppermute x1, waiting for transfers between devices, with_halo(): after = lax.ppermute(initial, axis, down)  3.41 us
  transfers between devices with their start and end apart: 3, of which 3 were waited for; matrix products, arithmetic and copies ran while one was open for 5% of the time, Pallas kernels for 0%

commit v1 on v0

v1 whole, which is shorter than its diff:
```python
import functools
import math

import jax
import jax.numpy as jnp
from jax import lax
from jax.experimental import pallas as pl
from jax.experimental.pallas import tpu as pltpu
from jax.sharding import PartitionSpec as P

HEADS = 16
MASKED = -1e30
F32 = jnp.float32
BF16 = jnp.bfloat16


def kernel(
    bands, rows_hbm, slot_ref, counts_ref, gain_ref, wqkv_hbm, wout_hbm, out_ref,
    rows, wqkv, wout, outgoing, arrived, halo, normed, query, keyval, mixed,
    load_sem, send_sem, recv_sem, halo_send, halo_recv,
):
    row_count, width = rows.shape
    cap = row_count // bands
    block = row_count // 4
    per_block = block // cap
    head_dim = width // HEADS
    me = lax.axis_index("band")

    loads = [
        pltpu.make_async_copy(source, target, load_sem.at[i])
        for i, (source, target) in enumerate(((rows_hbm, rows), (wqkv_hbm, wqkv), (wout_hbm, wout)))
    ]
    loads[0].start()

    barrier = pltpu.get_barrier_semaphore()

    def greet(step, carry):
        pl.semaphore_signal(barrier, inc=1, device_id={"band": lax.rem(me + step, bands)})
        return carry

    lax.fori_loop(1, bands, greet, 0)
    loads[0].wait()
    loads[1].start()
    loads[2].start()

    for j in range(4):
        slot_of = lax.broadcasted_iota(jnp.int32, (block, row_count), 0) + j * block
        onehot = (slot_of == slot_ref[...]).astype(BF16)
        placed = jnp.dot(onehot, rows[...], preferred_element_type=F32)
        outgoing[pl.ds(j * per_block, per_block)] = placed.reshape(per_block, cap, width).astype(BF16)
    arrived[pl.ds(me, 1)] = outgoing[pl.ds(me, 1)]

    def chunk(target, slot):
        return pltpu.make_async_remote_copy(
            src_ref=outgoing.at[target],
            dst_ref=arrived.at[slot],
            send_sem=send_sem.at[target],
            recv_sem=recv_sem.at[slot],
            device_id={"band": target},
        )

    pl.semaphore_wait(barrier, bands - 1)

    def send(step, carry):
        half = lax.div(step, 2)
        shift = bands // 2 + half * (1 - 2 * lax.rem(step, 2))
        chunk(lax.rem(me + shift, bands), me).start()
        return carry

    lax.fori_loop(1, bands, send, 0)

    def wait_block(j):
        def one(owner, carry):
            @pl.when(owner != me)
            def _():
                chunk(owner, owner).wait_recv()
            return carry

        lax.fori_loop(j * per_block, (j + 1) * per_block, one, 0)

    def edge(side, peer):
        return pltpu.make_async_remote_copy(
            src_ref=arrived.at[pl.ds(0 if side == 0 else 3 * per_block, per_block)],
            dst_ref=halo.at[1 - side],
            send_sem=halo_send.at[side],
            recv_sem=halo_recv.at[1 - side],
            device_id={"band": peer},
        )

    def normalize(chunks, first):
        values = chunks.astype(F32).reshape(block, width)
        center = jnp.mean(values, axis=-1, keepdims=True)
        values = values - center
        spread = jnp.mean(values * values, axis=-1, keepdims=True)
        normed[pl.ds(first, block)] = (values * lax.rsqrt(spread + 1e-05) * gain_ref[...]).astype(BF16)

    has_prev, has_next = me > 0, me < bands - 1
    wait_block(0)

    @pl.when(has_prev)
    def _():
        edge(0, me - 1).start()

    wait_block(3)

    @pl.when(has_next)
    def _():
        edge(1, me + 1).start()

    normalize(arrived[pl.ds(0, per_block)], block)
    normalize(arrived[pl.ds(3 * per_block, per_block)], 4 * block)
    wait_block(1)
    normalize(arrived[pl.ds(per_block, per_block)], 2 * block)
    wait_block(2)
    normalize(arrived[pl.ds(2 * per_block, per_block)], 3 * block)
    loads[1].wait()

    tile = width // 2
    factor = head_dim ** -0.5 * math.log2(math.e)

    def project_query(c, carry):
        columns = pl.ds(pl.multiple_of(c * tile, tile), tile)
        part = jnp.dot(normed[pl.ds(block, row_count)], wqkv[:, columns], preferred_element_type=F32)
        query[:, columns] = (part * factor).astype(BF16)
        return carry

    def project_keyval(first, count):
        def one(c, carry):
            columns = pl.ds(pl.multiple_of(c * tile, tile), tile)
            source = pl.ds(pl.multiple_of(c * tile + width, tile), tile)
            keyval[pl.ds(first, count), columns] = jnp.dot(
                normed[pl.ds(first, count)], wqkv[:, source], preferred_element_type=F32
            ).astype(BF16)
            return carry

        lax.fori_loop(0, 4, one, 0)

    lax.fori_loop(0, 2, project_query, 0)
    project_keyval(block, row_count)

    for side, there, peer in ((0, has_prev, me - 1), (1, has_next, me + 1)):
        @pl.when(there)
        def _(side=side, peer=peer):
            edge(1 - side, peer).wait_recv()

        @pl.when(jnp.logical_not(there))
        def _(side=side):
            halo[side] = jnp.zeros(halo.shape[1:], BF16)

        first = side * 5 * block
        normalize(halo[side], first)
        project_keyval(first, block)

    wide_count = row_count + 2 * block
    counts = counts_ref[...].astype(F32)
    band_lane = lax.broadcasted_iota(jnp.int32, (bands, bands), 1)

    def alive_row(band, owner_first, count):
        column = jnp.sum(jnp.where(band_lane == band, counts, 0.0), axis=1, keepdims=True)
        position = lax.broadcasted_iota(jnp.int32, (bands, count), 1) + owner_first * cap
        owner = lax.broadcasted_iota(jnp.int32, (bands, count), 0)
        here = jnp.sum(jnp.where(position // cap == owner, column, 0.0), axis=0, keepdims=True)
        number = (lax.broadcasted_iota(jnp.int32, (1, count), 1) % cap).astype(F32)
        return jnp.where(number < here, 0.0, MASKED)

    key_bias = jnp.concatenate(
        [alive_row(me - 1, 3 * per_block, block), alive_row(me, 0, row_count), alive_row(me + 1, 0, block)], axis=1
    )
    lane = lax.broadcasted_iota(jnp.int32, (1, 2 * head_dim), 1)
    first_head = lane < head_dim
    masks = [jnp.where(first_head, 1.0, 0.0).astype(BF16), jnp.where(first_head, 0.0, 1.0).astype(BF16)]
    key_at = lax.broadcasted_iota(jnp.int32, (block, 3 * block), 1)
    query_at = lax.broadcasted_iota(jnp.int32, (block, 3 * block), 0)
    within = (key_at >= query_at) & (key_at <= query_at + 2 * block)
    loads[2].wait()
    owner_of = lax.broadcasted_iota(jnp.int32, (block, bands), 0) // cap
    owner_lane = lax.broadcasted_iota(jnp.int32, (block, bands), 1)
    for j in range(4):
        queries = pl.ds(j * block, block)
        keys = pl.ds(j * block, 3 * block)
        bias = jnp.where(within, key_bias[:, j * block:(j + 3) * block], MASKED)

        def pair_of_heads(p, carry, queries=queries, keys=keys, bias=bias):
            columns = pl.ds(pl.multiple_of(p * 2 * head_dim, 2 * head_dim), 2 * head_dim)
            value_columns = pl.ds(pl.multiple_of(width + p * 2 * head_dim, 2 * head_dim), 2 * head_dim)
            both = query[queries, columns]
            stacked = jnp.concatenate([both * masks[0], both * masks[1]], axis=0)
            score = lax.dot_general(
                stacked, keyval[keys, columns], (((1,), (1,)), ((), ())), preferred_element_type=F32
            )
            score = score.reshape(2, block, 3 * block) + bias[None]
            weight = jnp.exp2(score - jnp.max(score, axis=-1, keepdims=True))
            total = jnp.sum(weight, axis=-1, keepdims=True)
            blended = jnp.dot(
                weight.reshape(2 * block, 3 * block).astype(BF16), keyval[keys, value_columns],
                preferred_element_type=F32,
            ).reshape(2, block, 2 * head_dim) / total
            mixed[:, columns] = jnp.where(first_head, blended[0], blended[1]).astype(BF16)
            return carry

        lax.fori_loop(0, HEADS // 2, pair_of_heads, 0, unroll=True)
        update = jnp.dot(mixed[...], wout[...], preferred_element_type=F32)
        spread_counts = jnp.dot(
            (owner_of + j * per_block == owner_lane).astype(F32), counts, preferred_element_type=F32
        )
        column = jnp.sum(jnp.where(owner_lane == me, spread_counts, 0.0), axis=1, keepdims=True)
        number = (lax.broadcasted_iota(jnp.int32, (block, 1), 0) % cap).astype(F32)
        out_ref[queries, :] = jnp.where(number < column, update, 0.0).astype(BF16)

    def sent(step, carry):
        chunk(lax.rem(me + step, bands), me).wait_send()
        return carry

    lax.fori_loop(1, bands, sent, 0)

    @pl.when(has_prev)
    def _():
        edge(0, me - 1).wait_send()

    @pl.when(has_next)
    def _():
        edge(1, me + 1).wait_send()


def body(grid_rows, row_slot, band_counts, norm_gain, w_qkv, w_out):
    row_count, width = grid_rows.shape
    bands = lax.axis_size("band")
    cap = row_count // bands
    block = row_count // 4
    vmem = pl.BlockSpec(memory_space=pltpu.VMEM)
    anywhere = pl.BlockSpec(memory_space=pl.ANY)
    return pl.pallas_call(
        functools.partial(kernel, bands),
        out_shape=jax.ShapeDtypeStruct((row_count, width), BF16),
        in_specs=[anywhere, vmem, vmem, vmem, anywhere, anywhere],
        out_specs=vmem,
        scratch_shapes=[
            pltpu.VMEM((row_count, width), BF16),
            pltpu.VMEM(w_qkv.shape, BF16),
            pltpu.VMEM(w_out.shape, BF16),
            pltpu.VMEM((bands, cap, width), BF16),
            pltpu.VMEM((bands, cap, width), BF16),
            pltpu.VMEM((2, block // cap, cap, width), BF16),
            pltpu.VMEM((row_count + 2 * block, width), BF16),
            pltpu.VMEM((row_count, width), BF16),
            pltpu.VMEM((row_count + 2 * block, 2 * width), BF16),
            pltpu.VMEM((block, width), BF16),
            pltpu.SemaphoreType.DMA((3,)),
            pltpu.SemaphoreType.DMA((bands,)),
            pltpu.SemaphoreType.DMA((bands,)),
            pltpu.SemaphoreType.DMA((2,)),
            pltpu.SemaphoreType.DMA((2,)),
        ],
        compiler_params=pltpu.CompilerParams(
            collective_id=0, has_side_effects=True, vmem_limit_bytes=48 * 1024 * 1024
        ),
    )(grid_rows, row_slot.reshape(1, row_count), band_counts, norm_gain.reshape(1, width), w_qkv, w_out)


def solution(mesh):
    return jax.shard_map(
        body,
        mesh=mesh,
        in_specs=(
            P(("groups", "band"), None),
            P(("groups", "band")),
            P("groups", None),
            P(),
            P(),
            P(),
        ),
        out_specs=P(("groups", "band"), None),
        check_vma=False,
    )
```

time: 121 us -> 53.8 us (0.44)
  the two profiles are of different devices: /device:TPU:19 before, /device:TPU:0 now
where the time goes in v1:
time: 53.8 us; the launch traced here: 53.6 us
  Pallas kernels  47.7 us (89%)
  local copies, waits for them, and re-layouts  5.85 us (11%)
    pallas_call x1, Pallas kernels, body(): pl.pallas_call(functools.partial(kernel, bands), out_shape=jax.ShapeDtype...  47.7 us
    unnamed x11, local copies, waits for them, and re-layouts  5.85 us

profile of v1, /device:TPU:0, one launch (start us, length us, event | category | flops | bytes accessed | tf_op | source)
XLA Modules:
  0.0 53.6 jit_solution(9778674360659667232)
XLA Ops:
  0.0 0.0 copy-start
  0.0 1.6 %copy-done = bf16[1024,1024]{1,0:T(8,128)(2,1)S(1)} copy-done((bf16[1024,1024]{1,0:T(8,128)(2,1)S(1)}, bf16[1024,1024]{1,0:T(8,128)(2,1)}, u32[]{:S(2)}) %copy-start) | copy-done | bytes 2097176
  1.6 0.0 copy-start.1
  1.6 1.2 %copy-done.1 = bf16[512,1024]{1,0:T(8,128)(2,1)S(1)} copy-done((bf16[512,1024]{1,0:T(8,128)(2,1)S(1)}, bf16[512,1024]{1,0:T(8,128)(2,1)}, u32[]{:S(2)}) %copy-start.1) | copy-done | bytes 1048600
  2.8 0.0 copy-start.2
  2.8 0.7 %copy-done.2 = s32[16,16]{1,0:T(8,128)S(1)} copy-done((s32[16,16]{1,0:T(8,128)S(1)}, s32[16,16]{1,0:T(8,128)}, u32[]{:S(2)}) %copy-start.2) | copy-done | bytes 1048
  3.5 0.0 copy-start.3
  3.5 0.7 %copy-done.3 = f32[1024]{0:T(1024)S(1)} copy-done((f32[1024]{0:T(1024)S(1)}, f32[1024]{0:T(1024)}, u32[]{:S(2)}) %copy-start.3) | copy-done | bytes 4120
  4.2 0.0 copy-start.4
  4.2 0.7 %copy-done.4 = s32[512]{0:T(512)S(1)} copy-done((s32[512]{0:T(512)S(1)}, s32[512]{0:T(512)}, u32[]{:S(2)}) %copy-start.4) | copy-done | bytes 2072
  4.9 47.7 %shard_map.64 = bf16[512,1024]{1,0:T(8,128)(2,1)S(1)} custom-call(bf16[512,1024]{1,0:T(8,128)(2,1)S(1)} %copy-done.1, s32[1,512]{1,0:T(1,128)S(1)} %bitcast.3, s32[16,16]{1,0:T(8,128)S(1)} %copy-done.2, f32[1,1024]{1,0:T(1,128)S(1)} %bitcast.2, bf16[1024,3072]{1,0:T(8,128)(2,1)} %wqkv_hbm.1, bf16[1024,1024]{1,0:T(8,128)(2,1)S(1)} %copy-done), custom_call_target="tpu_custom_call" | custom-call | tf_op jit(solution)/shard_map/pallas_call | solution.py:232
  52.6 1.0 %copy.8 = bf16[512,1024]{1,0:T(8,128)(2,1)} copy(bf16[512,1024]{1,0:T(8,128)(2,1)S(1)} %shard_map.64) | data formatting | bytes 2097152
Async XLA Ops:
  0.0 1.6 %copy-start = (bf16[1024,1024]{1,0:T(8,128)(2,1)S(1)}, bf16[1024,1024]{1,0:T(8,128)(2,1)}, u32[]{:S(2)}) copy-start(bf16[1024,1024]{1,0:T(8,128)(2,1)} %wout_hbm.1) | copy-start | bytes 6291460
  1.6 1.2 %copy-start.1 = (bf16[512,1024]{1,0:T(8,128)(2,1)S(1)}, bf16[512,1024]{1,0:T(8,128)(2,1)}, u32[]{:S(2)}) copy-start(bf16[512,1024]{1,0:T(8,128)(2,1)} %rows_hbm.1) | copy-start | bytes 3145732
  2.8 0.7 %copy-start.2 = (s32[16,16]{1,0:T(8,128)S(1)}, s32[16,16]{1,0:T(8,128)}, u32[]{:S(2)}) copy-start(s32[16,16]{1,0:T(8,128)} %counts_ref.1) | copy-start | bytes 3076
  3.5 0.7 %copy-start.3 = (f32[1024]{0:T(1024)S(1)}, f32[1024]{0:T(1024)}, u32[]{:S(2)}) copy-start(f32[1024]{0:T(1024)} %param.9) | copy-start | bytes 12292
  4.2 0.7 %copy-start.4 = (s32[512]{0:T(512)S(1)}, s32[512]{0:T(512)}, u32[]{:S(2)}) copy-start(s32[512]{0:T(512)} %param.7) | copy-start | bytes 6148

commit v2 on v1

v2 whole, which is shorter than its diff:
```python
import functools
import math

import jax
import jax.numpy as jnp
from jax import lax
from jax.experimental import pallas as pl
from jax.experimental.pallas import tpu as pltpu
from jax.sharding import PartitionSpec as P

HEADS = 16
MASKED = -1e30
F32 = jnp.float32
BF16 = jnp.bfloat16


def kernel(
    bands, rows_hbm, slot_hbm, counts_hbm, gain_hbm, wqkv_hbm, wout_hbm, out_ref,
    rows, slot_ref, counts_ref, gain_ref, wqkv, wout, outgoing, arrived, halo, normed, query, keyval, mixed,
    load_sem, send_sem, recv_sem, halo_send, halo_recv,
):
    row_count, width = rows.shape
    cap = row_count // bands
    block = row_count // 4
    per_block = block // cap
    head_dim = width // HEADS
    me = lax.axis_index("band")

    loads = [
        pltpu.make_async_copy(source, target, load_sem.at[i])
        for i, (source, target) in enumerate((
            (slot_hbm, slot_ref), (rows_hbm, rows), (gain_hbm, gain_ref), (counts_hbm, counts_ref),
            (wqkv_hbm, wqkv), (wout_hbm, wout),
        ))
    ]
    for load in loads:
        load.start()

    barrier = pltpu.get_barrier_semaphore()

    def greet(step, carry):
        pl.semaphore_signal(barrier, inc=1, device_id={"band": lax.rem(me + step, bands)})
        return carry

    lax.fori_loop(1, bands, greet, 0)
    loads[0].wait()
    loads[1].wait()

    quarter = me // per_block
    ascending = quarter % 2 == 1

    def chunk(target, slot):
        return pltpu.make_async_remote_copy(
            src_ref=outgoing.at[target],
            dst_ref=arrived.at[slot],
            send_sem=send_sem.at[target],
            recv_sem=recv_sem.at[slot],
            device_id={"band": target},
        )

    for step in range(4):
        part = jnp.where(ascending, step, 3 - step)
        slot_of = lax.broadcasted_iota(jnp.int32, (block, row_count), 0) + part * block
        onehot = (slot_of == slot_ref[...]).astype(BF16)
        placed = jnp.dot(onehot, rows[...], preferred_element_type=F32)
        outgoing[pl.ds(part * per_block, per_block)] = placed.reshape(per_block, cap, width).astype(BF16)
        if step == 0:
            pl.semaphore_wait(barrier, bands - 1)

        def send(i, carry, part=part):
            target = part * per_block + (me + i) % per_block

            @pl.when(target != me)
            def _():
                chunk(target, me).start()

            return carry

        lax.fori_loop(0, per_block, send, 0)
    arrived[pl.ds(me, 1)] = outgoing[pl.ds(me, 1)]

    def wait_block(j):
        def one(i, carry):
            owner = j * per_block + i

            @pl.when(owner != me)
            def _():
                chunk(owner, owner).wait_recv()
            return carry

        lax.fori_loop(0, per_block, one, 0)

    def edge(side, peer):
        return pltpu.make_async_remote_copy(
            src_ref=arrived.at[pl.ds(0 if side == 0 else 3 * per_block, per_block)],
            dst_ref=halo.at[1 - side],
            send_sem=halo_send.at[side],
            recv_sem=halo_recv.at[1 - side],
            device_id={"band": peer},
        )

    def normalize(chunks, place):
        values = chunks.astype(F32).reshape(block, width)
        center = jnp.mean(values, axis=-1, keepdims=True)
        values = values - center
        spread = jnp.mean(values * values, axis=-1, keepdims=True)
        normed[pl.ds(place * block, block)] = (values * lax.rsqrt(spread + 1e-05) * gain_ref[...]).astype(BF16)

    tile = width // 2
    factor = head_dim ** -0.5 * math.log2(math.e)

    def project_query(place, count, blocks):
        def one(c, carry):
            columns = pl.ds(pl.multiple_of(c * tile, tile), tile)
            part = jnp.dot(normed[pl.ds(place * block, count * block)], wqkv[:, columns], preferred_element_type=F32)
            part = (part * factor).astype(BF16)
            for i, at in enumerate(blocks):
                query[pl.ds(pl.multiple_of(at * block, block), block), columns] = part[i * block:(i + 1) * block]
            return carry

        lax.fori_loop(0, 2, one, 0)

    def project_keyval(place, count, blocks):
        def one(c, carry):
            columns = pl.ds(pl.multiple_of(c * tile, tile), tile)
            source = pl.ds(pl.multiple_of(c * tile + width, tile), tile)
            part = jnp.dot(normed[pl.ds(place * block, count * block)], wqkv[:, source], preferred_element_type=F32)
            part = part.astype(BF16)
            for i, at in enumerate(blocks):
                keyval[pl.ds(pl.multiple_of((at + 1) * block, block), block), columns] = part[i * block:(i + 1) * block]
            return carry

        lax.fori_loop(0, 4, one, 0)

    upper = quarter // 2
    near_inner, near_outer = 1 + upper, 3 * upper
    far_outer, far_inner = 3 - 3 * upper, 2 - upper
    has_prev, has_next = me > 0, me < bands - 1

    def arrived_block(j):
        return arrived[pl.ds(j * per_block, per_block)]

    def pass_on(j):
        @pl.when((j == 0) & has_prev)
        def _():
            edge(0, me - 1).start()

        @pl.when((j == 3) & has_next)
        def _():
            edge(1, me + 1).start()

    loads[2].wait()
    loads[3].wait()
    loads[4].wait()
    wait_block(near_inner)
    normalize(arrived_block(near_inner), 0)
    project_query(0, 1, (near_inner,))
    project_keyval(0, 1, (near_inner,))
    wait_block(near_outer)
    pass_on(near_outer)
    wait_block(far_outer)
    pass_on(far_outer)
    normalize(arrived_block(near_outer), 1)
    normalize(arrived_block(far_outer), 2)
    project_query(1, 2, (near_outer, far_outer))
    project_keyval(1, 2, (near_outer, far_outer))
    for side, there, peer in ((0, has_prev, me - 1), (1, has_next, me + 1)):
        @pl.when(there)
        def _(side=side, peer=peer):
            edge(1 - side, peer).wait_recv()

        @pl.when(jnp.logical_not(there))
        def _(side=side):
            halo[side] = jnp.zeros(halo.shape[1:], BF16)

        normalize(halo[side], 3 + side)
    wait_block(far_inner)
    normalize(arrived_block(far_inner), 5)
    project_query(5, 1, (far_inner,))
    project_keyval(3, 3, (-1, 4, far_inner))

    wide_count = row_count + 2 * block
    counts = counts_ref[...].astype(F32)
    band_lane = lax.broadcasted_iota(jnp.int32, (bands, bands), 1)

    def alive_row(band, owner_first, count):
        column = jnp.sum(jnp.where(band_lane == band, counts, 0.0), axis=1, keepdims=True)
        position = lax.broadcasted_iota(jnp.int32, (bands, count), 1) + owner_first * cap
        owner = lax.broadcasted_iota(jnp.int32, (bands, count), 0)
        here = jnp.sum(jnp.where(position // cap == owner, column, 0.0), axis=0, keepdims=True)
        number = (lax.broadcasted_iota(jnp.int32, (1, count), 1) % cap).astype(F32)
        return jnp.where(number < here, 0.0, MASKED)

    key_bias = jnp.concatenate(
        [alive_row(me - 1, 3 * per_block, block), alive_row(me, 0, row_count), alive_row(me + 1, 0, block)], axis=1
    )
    lane = lax.broadcasted_iota(jnp.int32, (1, 2 * head_dim), 1)
    first_head = lane < head_dim
    masks = [jnp.where(first_head, 1.0, 0.0).astype(BF16), jnp.where(first_head, 0.0, 1.0).astype(BF16)]
    key_at = lax.broadcasted_iota(jnp.int32, (block, 3 * block), 1)
    query_at = lax.broadcasted_iota(jnp.int32, (block, 3 * block), 0)
    within = (key_at >= query_at) & (key_at <= query_at + 2 * block)
    loads[5].wait()
    owner_of = lax.broadcasted_iota(jnp.int32, (block, bands), 0) // cap
    owner_lane = lax.broadcasted_iota(jnp.int32, (block, bands), 1)
    for j in range(4):
        queries = pl.ds(j * block, block)
        keys = pl.ds(j * block, 3 * block)
        bias = jnp.where(within, key_bias[:, j * block:(j + 3) * block], MASKED)

        def score_of(p, queries=queries, keys=keys):
            columns = slice(p * 2 * head_dim, (p + 1) * 2 * head_dim)
            key = keyval[keys, columns]
            return lax.dot_general(
                query[queries, columns], jnp.concatenate([key * masks[0], key * masks[1]], axis=0),
                (((1,), (1,)), ((), ())), preferred_element_type=F32,
            )

        score = score_of(0)
        for p in range(HEADS // 2):
            later = score_of(p + 1) if p + 1 < HEADS // 2 else None
            weights = []
            for h in range(2):
                own = score[:, h * 3 * block:(h + 1) * 3 * block] + bias
                weights.append(jnp.exp2(own - jnp.max(own, axis=-1, keepdims=True)).astype(BF16))
            value = keyval[keys, width + p * 2 * head_dim:width + (p + 1) * 2 * head_dim]
            blended = jnp.dot(
                jnp.concatenate(weights, axis=1),
                jnp.concatenate([
                    jnp.concatenate([value * mask, jnp.broadcast_to(mask, value.shape)], axis=1) for mask in masks
                ], axis=0),
                preferred_element_type=F32,
            )
            mixed[:, p * 2 * head_dim:(p + 1) * 2 * head_dim] = (
                blended[:, :2 * head_dim] / blended[:, 2 * head_dim:]
            ).astype(BF16)
            score = later

        update = jnp.dot(mixed[...], wout[...], preferred_element_type=F32)
        spread_counts = jnp.dot(
            (owner_of + j * per_block == owner_lane).astype(F32), counts, preferred_element_type=F32
        )
        column = jnp.sum(jnp.where(owner_lane == me, spread_counts, 0.0), axis=1, keepdims=True)
        number = (lax.broadcasted_iota(jnp.int32, (block, 1), 0) % cap).astype(F32)
        out_ref[queries, :] = jnp.where(number < column, update, 0.0).astype(BF16)

    def sent(step, carry):
        chunk(lax.rem(me + step, bands), me).wait_send()
        return carry

    lax.fori_loop(1, bands, sent, 0)

    @pl.when(has_prev)
    def _():
        edge(0, me - 1).wait_send()

    @pl.when(has_next)
    def _():
        edge(1, me + 1).wait_send()


def body(grid_rows, row_slot, band_counts, norm_gain, w_qkv, w_out):
    row_count, width = grid_rows.shape
    bands = lax.axis_size("band")
    cap = row_count // bands
    block = row_count // 4
    vmem = pl.BlockSpec(memory_space=pltpu.VMEM)
    hbm = pl.BlockSpec(memory_space=pltpu.HBM)
    return pl.pallas_call(
        functools.partial(kernel, bands),
        out_shape=jax.ShapeDtypeStruct((row_count, width), BF16),
        in_specs=[hbm] * 6,
        out_specs=vmem,
        scratch_shapes=[
            pltpu.VMEM((row_count, width), BF16),
            pltpu.VMEM((1, row_count), jnp.int32),
            pltpu.VMEM((bands, bands), jnp.int32),
            pltpu.VMEM((1, width), F32),
            pltpu.VMEM(w_qkv.shape, BF16),
            pltpu.VMEM(w_out.shape, BF16),
            pltpu.VMEM((bands, cap, width), BF16),
            pltpu.VMEM((bands, cap, width), BF16),
            pltpu.VMEM((2, block // cap, cap, width), BF16),
            pltpu.VMEM((row_count + 2 * block, width), BF16),
            pltpu.VMEM((row_count, width), BF16),
            pltpu.VMEM((row_count + 2 * block, 2 * width), BF16),
            pltpu.VMEM((block, width), BF16),
            pltpu.SemaphoreType.DMA((6,)),
            pltpu.SemaphoreType.DMA((bands,)),
            pltpu.SemaphoreType.DMA((bands,)),
            pltpu.SemaphoreType.DMA((2,)),
            pltpu.SemaphoreType.DMA((2,)),
        ],
        compiler_params=pltpu.CompilerParams(
            collective_id=0, has_side_effects=True, vmem_limit_bytes=64 * 1024 * 1024
        ),
    )(grid_rows, row_slot.reshape(1, row_count), band_counts, norm_gain.reshape(1, width), w_qkv, w_out)


def solution(mesh):
    return jax.shard_map(
        body,
        mesh=mesh,
        in_specs=(
            P(("groups", "band"), None),
            P(("groups", "band")),
            P("groups", None),
            P(),
            P(),
            P(),
        ),
        out_specs=P(("groups", "band"), None),
        check_vma=False,
    )
```

time: 53.8 us -> 45.1 us (0.84)
  the two profiles are of different devices: /device:TPU:0 before, /device:TPU:5 now
where the time goes in v2:
time: 45.1 us; the launch traced here: 44.9 us
  Pallas kernels  42.6 us (94%)
  local copies, waits for them, and re-layouts  2.26 us (5%)
    pallas_call x1, Pallas kernels, body(): pl.pallas_call(functools.partial(kernel, bands), out_shape=jax.ShapeDtype...  42.6 us
    unnamed x1, local copies, waits for them, and re-layouts  2.26 us

profile of v2, /device:TPU:5, one launch (start us, length us, event | category | flops | bytes accessed | tf_op | source)
XLA Modules:
  0.0 44.9 jit_solution(3640851843426733239)
XLA Ops:
  0.0 42.6 %shard_map.64 = bf16[512,1024]{1,0:T(8,128)(2,1)} custom-call(bf16[512,1024]{1,0:T(8,128)(2,1)} %rows_hbm.1, s32[1,512]{1,0:T(1,128)} %bitcast.3, s32[16,16]{1,0:T(8,128)} %counts_hbm.1, f32[1,1024]{1,0:T(1,128)} %bitcast.2, bf16[1024,3072]{1,0:T(8,128)(2,1)} %wqkv_hbm.1, bf16[1024,1024]{1,0:T(8,128)(2,1)} %wout_hbm.1), custom_call_target="tpu_custom_call" | custom-call | tf_op jit(solution)/shard_map/pallas_call | solution.py:269
  42.6 2.3 %copy.8 = bf16[512,1024]{1,0:T(8,128)(2,1)} copy(bf16[512,1024]{1,0:T(8,128)(2,1)} %shard_map.64) | data formatting | bytes 2097152

commit v3 on v2

--- a/solution.py
+++ b/solution.py
@@ -79,23 +79,12 @@
         lax.fori_loop(0, per_block, send, 0)
     arrived[pl.ds(me, 1)] = outgoing[pl.ds(me, 1)]
 
-    def wait_block(j):
-        def one(i, carry):
-            owner = j * per_block + i
-
-            @pl.when(owner != me)
-            def _():
-                chunk(owner, owner).wait_recv()
-            return carry
-
-        lax.fori_loop(0, per_block, one, 0)
-
-    def edge(side, peer):
+    def edge(side, i, peer):
         return pltpu.make_async_remote_copy(
-            src_ref=arrived.at[pl.ds(0 if side == 0 else 3 * per_block, per_block)],
-            dst_ref=halo.at[1 - side],
-            send_sem=halo_send.at[side],
-            recv_sem=halo_recv.at[1 - side],
+            src_ref=arrived.at[(0 if side == 0 else 3 * per_block) + i],
+            dst_ref=halo.at[1 - side, i],
+            send_sem=halo_send.at[side, i],
+            recv_sem=halo_recv.at[1 - side, i],
             device_id={"band": peer},
         )
 
@@ -140,14 +129,29 @@
     def arrived_block(j):
         return arrived[pl.ds(j * per_block, per_block)]
 
-    def pass_on(j):
-        @pl.when((j == 0) & has_prev)
-        def _():
-            edge(0, me - 1).start()
-
-        @pl.when((j == 3) & has_next)
-        def _():
-            edge(1, me + 1).start()
+    def wait_block(j, pass_on=False):
+        def one(i, carry):
+            owner = j * per_block + i
+
+            @pl.when(owner != me)
+            def _():
+                chunk(owner, owner).wait_recv()
+
+            if pass_on:
+                @pl.when((j == 0) & has_prev)
+                def _():
+                    edge(0, i, me - 1).start()
+
+                @pl.when((j == 3) & has_next)
+                def _():
+                    edge(1, i, me + 1).start()
+
+            return carry
+
+        lax.fori_loop(0, per_block, one, 0)
+
+    def each_edge(act):
+        lax.fori_loop(0, per_block, lambda i, carry: (act(i), carry)[1], 0)
 
     loads[2].wait()
     loads[3].wait()
@@ -156,28 +160,27 @@
     normalize(arrived_block(near_inner), 0)
     project_query(0, 1, (near_inner,))
     project_keyval(0, 1, (near_inner,))
-    wait_block(near_outer)
-    pass_on(near_outer)
-    wait_block(far_outer)
-    pass_on(far_outer)
+    wait_block(near_outer, pass_on=True)
+    wait_block(far_outer, pass_on=True)
     normalize(arrived_block(near_outer), 1)
     normalize(arrived_block(far_outer), 2)
     project_query(1, 2, (near_outer, far_outer))
     project_keyval(1, 2, (near_outer, far_outer))
+    wait_block(far_inner)
+    normalize(arrived_block(far_inner), 5)
+    project_query(5, 1, (far_inner,))
+    project_keyval(5, 1, (far_inner,))
     for side, there, peer in ((0, has_prev, me - 1), (1, has_next, me + 1)):
         @pl.when(there)
         def _(side=side, peer=peer):
-            edge(1 - side, peer).wait_recv()
+            each_edge(lambda i: edge(1 - side, i, peer).wait_recv())
 
         @pl.when(jnp.logical_not(there))
         def _(side=side):
             halo[side] = jnp.zeros(halo.shape[1:], BF16)
 
         normalize(halo[side], 3 + side)
-    wait_block(far_inner)
-    normalize(arrived_block(far_inner), 5)
-    project_query(5, 1, (far_inner,))
-    project_keyval(3, 3, (-1, 4, far_inner))
+    project_keyval(3, 2, (-1, 4))
 
     wide_count = row_count + 2 * block
     counts = counts_ref[...].astype(F32)
@@ -203,6 +206,7 @@
     loads[5].wait()
     owner_of = lax.broadcasted_iota(jnp.int32, (block, bands), 0) // cap
     owner_lane = lax.broadcasted_iota(jnp.int32, (block, bands), 1)
+    alive = []
     for j in range(4):
         queries = pl.ds(j * block, block)
         keys = pl.ds(j * block, 3 * block)
@@ -231,18 +235,24 @@
                 ], axis=0),
                 preferred_element_type=F32,
             )
-            mixed[:, p * 2 * head_dim:(p + 1) * 2 * head_dim] = (
+            mixed[queries, p * 2 * head_dim:(p + 1) * 2 * head_dim] = (
                 blended[:, :2 * head_dim] / blended[:, 2 * head_dim:]
             ).astype(BF16)
             score = later
 
-        update = jnp.dot(mixed[...], wout[...], preferred_element_type=F32)
         spread_counts = jnp.dot(
             (owner_of + j * per_block == owner_lane).astype(F32), counts, preferred_element_type=F32
         )
         column = jnp.sum(jnp.where(owner_lane == me, spread_counts, 0.0), axis=1, keepdims=True)
         number = (lax.broadcasted_iota(jnp.int32, (block, 1), 0) % cap).astype(F32)
-        out_ref[queries, :] = jnp.where(number < column, update, 0.0).astype(BF16)
+        alive.append(number < column)
+
+    for c in range(2):
+        columns = slice(c * tile, (c + 1) * tile)
+        update = jnp.dot(mixed[...], wout[:, columns], preferred_element_type=F32)
+        for j in range(4):
+            queries = slice(j * block, (j + 1) * block)
+            out_ref[queries, columns] = jnp.where(alive[j], update[queries], 0.0).astype(BF16)
 
     def sent(step, carry):
         chunk(lax.rem(me + step, bands), me).wait_send()
@@ -252,11 +262,11 @@
 
     @pl.when(has_prev)
     def _():
-        edge(0, me - 1).wait_send()
+        each_edge(lambda i: edge(0, i, me - 1).wait_send())
 
     @pl.when(has_next)
     def _():
-        edge(1, me + 1).wait_send()
+        each_edge(lambda i: edge(1, i, me + 1).wait_send())
 
 
 def body(grid_rows, row_slot, band_counts, norm_gain, w_qkv, w_out):
@@ -284,12 +294,12 @@
             pltpu.VMEM((row_count + 2 * block, width), BF16),
             pltpu.VMEM((row_count, width), BF16),
             pltpu.VMEM((row_count + 2 * block, 2 * width), BF16),
-            pltpu.VMEM((block, width), BF16),
+            pltpu.VMEM((row_count, width), BF16),
             pltpu.SemaphoreType.DMA((6,)),
             pltpu.SemaphoreType.DMA((bands,)),
             pltpu.SemaphoreType.DMA((bands,)),
-            pltpu.SemaphoreType.DMA((2,)),
-            pltpu.SemaphoreType.DMA((2,)),
+            pltpu.SemaphoreType.DMA((2, block // cap)),
+            pltpu.SemaphoreType.DMA((2, block // cap)),
         ],
         compiler_params=pltpu.CompilerParams(
             collective_id=0, has_side_effects=True, vmem_limit_bytes=64 * 1024 * 1024

time: 45.1 us -> 44.7 us (level)
  the two profiles are of different devices: /device:TPU:5 before, /device:TPU:0 now
where the time goes in v3:
time: 44.7 us; the launch traced here: 44.5 us
  Pallas kernels  42.2 us (94%)
  local copies, waits for them, and re-layouts  2.26 us (5%)
    pallas_call x1, Pallas kernels, body(): pl.pallas_call(functools.partial(kernel, bands), out_shape=jax.ShapeDtype...  42.2 us
    unnamed x1, local copies, waits for them, and re-layouts  2.26 us

profile of v3, /device:TPU:0, one launch (start us, length us, event | category | flops | bytes accessed | tf_op | source)
XLA Modules:
  0.0 44.5 jit_solution(17155905113599481925)
XLA Ops:
  0.0 42.2 %shard_map.64 = bf16[512,1024]{1,0:T(8,128)(2,1)} custom-call(bf16[512,1024]{1,0:T(8,128)(2,1)} %rows_hbm.1, s32[1,512]{1,0:T(1,128)} %bitcast.3, s32[16,16]{1,0:T(8,128)} %counts_hbm.1, f32[1,1024]{1,0:T(1,128)} %bitcast.2, bf16[1024,3072]{1,0:T(8,128)(2,1)} %wqkv_hbm.1, bf16[1024,1024]{1,0:T(8,128)(2,1)} %wout_hbm.1), custom_call_target="tpu_custom_call" | custom-call | tf_op jit(solution)/shard_map/pallas_call | solution.py:279
  42.2 2.3 %copy.8 = bf16[512,1024]{1,0:T(8,128)(2,1)} copy(bf16[512,1024]{1,0:T(8,128)(2,1)} %shard_map.64) | data formatting | bytes 2097152
